TPU v7x, 512 devices: a whole 4x4x16 slice. The times are simulated.
512 devices in a mesh: row: 8 (over x, y_lo), col: 16 (over z), dp: 4 (over y_hi, core).
Axes of the slice: x: 4, y: 4 (y_hi: 2, y_lo: 2; y = y_hi * 2 + y_lo), z: 16, core: 2. Of those that a mesh axis runs over, the one named last changes fastest.
Arguments:
- tokens: bfloat16 [512, 16384], P('dp', 'col'), may hold values from -6 to 6
- block_values: bfloat16 [8, 16, 32, 128, 128], P('row', 'col'), may hold values from -0.21875 to 0.21875
- block_index: int32 [8, 16, 2, 32], P('row', 'col'), may hold values from 0 to 31, as said below
- block_count: int32 [8, 16], P('row', 'col'), may hold values from 4 to 32, as said below
- grad_hidden: bfloat16 [512, 32768], P('dp', ('row', 'col')), may hold values from -3 to 3
Outputs:
- hidden: bfloat16 [512, 32768], P('dp', ('row', 'col'))
- grad_tokens: bfloat16 [512, 16384], P('dp', ('col', 'row'))
- grad_blocks: bfloat16 [8, 16, 32, 128, 128], P('row', 'col', 'dp')
Inputs may be any that keep to these rules, and one draw needn't show every extreme that they name: block_index[r, c, 0, s] is a block row below 32 and block_index[r, c, 1, s] a block column below 8 inside cell (r, c); the live slots of a cell name distinct positions; slots at or past block_count[r, c] are unused. `block_count`: some cell holds exactly 32 live slots in every draw.
All inputs are finite; a program needn't handle non-finite values.
Results may differ from a plain program's by a relative error of at most 0.017.
Values may be sent and summed in bfloat16 or wider, within the bound.
No kernel may reach another device: no remote copies, remote signals or barrier semaphores. Data moves between devices by JAX's collectives and lax.ppermute only.
A program may use at most 64 MiB of HBM per device.

v0:
```python
import jax
import jax.numpy as jnp
from jax import lax
from jax.sharding import PartitionSpec as P

grad_scale = 0.0625


def masked_total(make_terms, segment_ids, live_slots, segments):
    capacity = segment_ids.shape[0]
    slot_terms = jnp.where(live_slots[:, None, None], make_terms(0, capacity), 0.0)
    return jax.ops.segment_sum(slot_terms, segment_ids, num_segments=segments)


def local(tokens, block_values, block_index, block_count, grad_hidden):
    weight_blocks = block_values[0, 0]
    block_rows = block_index[0, 0, 0]
    block_cols = block_index[0, 0, 1]
    live_count = block_count[0, 0]
    capacity = weight_blocks.shape[0]
    block_size = weight_blocks.shape[1]
    token_count = tokens.shape[0]
    col_blocks = tokens.shape[1] // block_size
    piece_blocks = grad_hidden.shape[1] // block_size
    col_devices = lax.axis_size("col")
    dp_devices = lax.axis_size("dp")
    row_blocks = piece_blocks * col_devices
    live_slots = jnp.arange(capacity) < live_count
    token_blocks = tokens.reshape(token_count, col_blocks, block_size)

    def forward_terms(first_slot, number):
        chosen = jnp.take(token_blocks, block_cols, axis=1)
        return jnp.einsum("tsm,snm->stn", chosen, weight_blocks, preferred_element_type=jnp.float32)

    hidden_blocks = masked_total(forward_terms, block_rows, live_slots, row_blocks)
    hidden_part = hidden_blocks.transpose(1, 0, 2).reshape(token_count, row_blocks * block_size)
    hidden = lax.psum_scatter(
        hidden_part.astype(jnp.bfloat16), "col", scatter_dimension=1, tiled=True
    )
    dp_index = lax.axis_index("dp")
    owned_slots = capacity // dp_devices
    own_first = dp_index * owned_slots
    own_live = lax.dynamic_slice_in_dim(live_slots, own_first, owned_slots)
    local_rows = lax.all_gather(grad_hidden, "col", axis=1, tiled=True).reshape(
        token_count, row_blocks, block_size
    )

    def grad_terms(first_slot, number):
        picked = jnp.take(local_rows, block_rows, axis=1)
        return jnp.einsum("tsn,snm->stm", picked, weight_blocks, preferred_element_type=jnp.float32)

    grad_pick = jnp.take(local_rows, block_rows, axis=1)
    token_pick = jnp.take(token_blocks, block_cols, axis=1)
    slot_partial = jnp.einsum(
        "tsn,tsm->snm", grad_pick, token_pick, preferred_element_type=jnp.float32
    )
    weight_sums = lax.psum_scatter(
        slot_partial.astype(jnp.bfloat16), "dp", scatter_dimension=0, tiled=True
    ).astype(jnp.float32)
    feature_blocks = masked_total(grad_terms, block_cols, live_slots, col_blocks)
    feature_part = feature_blocks.transpose(1, 0, 2).reshape(token_count, col_blocks * block_size)
    grad_tokens = lax.psum_scatter(
        feature_part.astype(jnp.bfloat16), "row", scatter_dimension=1, tiled=True
    )
    grad_blocks = jnp.where(own_live[:, None, None], weight_sums * grad_scale, 0.0).astype(
        jnp.bfloat16
    )
    return (hidden, grad_tokens, grad_blocks[None, None])


def solution(mesh):
    in_specs = (
        P("dp", "col"),
        P("row", "col", None, None, None),
        P("row", "col", None, None),
        P("row", "col"),
        P("dp", ("row", "col")),
    )
    out_specs = (
        P("dp", ("row", "col")),
        P("dp", ("col", "row")),
        P("row", "col", "dp", None, None),
    )
    return jax.shard_map(local, mesh=mesh, in_specs=in_specs, out_specs=out_specs, check_vma=False)
```

profile of v0, /device:TPU:1, one launch (start us, length us, event | category | flops | bytes accessed | tf_op | source)
XLA Modules:
  0.0 260.6 jit_solution(12291143587485037593)
XLA Ops:
  7.2 0.0 copy-start
  7.2 0.0 copy-start.4
  7.2 0.0 all-gather.2.cloned.1.call-start
  7.2 1.6 copy.17
  8.9 0.0 all-gather.2.cloned.1.call-update
  8.9 0.0 reduce-scatter.4.cloned.1.call-start
  9.6 1.1 copy.14
  10.7 0.2 copy.15
  10.9 0.8 compare_and_fusion
  11.7 0.7 gather_fusion
  12.5 0.0 copy-start.1
  12.5 0.0 copy-done.4
  12.5 0.0 copy-done
  12.5 2.2 convolution_select_fusion.1
  14.7 0.0 copy-done.1
  14.8 0.2 broadcast_in_dim.54
  15.0 4.7 %scatter_fusion = f32[32,128,128]{2,1,0:T(8,128)S(1)} fusion(f32[32,128,128]{2,1,0:T(8,128)S(1)} %broadcast_in_dim.54, s32[32]{0:T(128)S(1)} %get-tuple-element.18, f32[32,128,128]{2,1,0:T(8,128)} %convolution_select_fusion.1), kind=kCustom, calls=%fused_computation.2 | custom fusion | flops 524288 | bytes 6291584 | tf_op jit(solution)/shard_map/scatter-add | solution.py:12
  19.7 1.1 convert_bitcast_fusion
  20.8 2.3 copy.16
  23.1 0.0 reduce-scatter.4.cloned.1.call-update
  23.1 0.0 reduce-scatter.6.cloned.1.call-start
  23.1 54.4 %all-gather.2.cloned.1.call-done = bf16[128,4096]{0,1:T(8,128)(2,1)} async-done(((bf16[128,256]{0,1:T(8,128)(2,1)}), bf16[128,4096]{0,1:T(8,128)(2,1)}) %all-gather.2.cloned.1.call-update) | async-done | bytes 1048592 | tf_op jit(solution)/shard_map/all_gather | solution.py:44
  77.6 1.6 copy.18
  79.2 0.7 gather_fusion.1
  80.0 0.0 copy-start.3
  80.0 1.8 convolution_select_fusion
  81.8 0.0 copy-done.3
  81.9 0.0 copy-start.2
  81.9 4.7 %scatter_fusion.1 = f32[8,128,128]{2,1,0:T(8,128)S(1)} fusion(f32[8,128,128]{2,1,0:T(8,128)S(1)} %broadcast_in_dim.56, s32[32]{0:T(128)S(1)} %get-tuple-element.17, f32[32,128,128]{2,1,0:T(8,128)} %convolution_select_fusion), kind=kCustom, calls=%fused_computation.3 | custom fusion | flops 524288 | bytes 6291584 | tf_op jit(solution)/shard_map/scatter-add | solution.py:12
  86.6 0.9 copy.19
  87.4 0.0 reduce-scatter.6.cloned.1.call-update
  87.5 0.0 reduce-scatter.8.cloned.1.call-start
  87.5 0.0 copy-done.2
  87.5 2.8 %convolution_convert_fusion = bf16[32,128,128]{2,1,0:T(8,128)(2,1)} fusion(bf16[32,128,128]{2,1,0:T(8,128)(2,1)S(1)} %copy-done.2, pred[32]{0:T(512)(128)(4,1)S(1)} %get-tuple-element.15, bf16[32,128,128]{2,1,0:T(8,128)(2,1)} %copy-done.3, pred[32]{0:T(512)(128)(4,1)S(1)} %get-tuple-element.11), kind=kOutput, calls=%fused_computation.6 | convolution fusion | flops 135790592 | bytes 3145792 | tf_op jit(solution)/shard_map/tsn,tsm->snm/dot_general | solution.py:54
  90.3 0.0 reduce-scatter.8.cloned.1.call-update
  90.3 0.1 dynamic_slice.3
  90.4 56.6 %reduce-scatter.4.cloned.1.call-done = bf16[128,256]{0,1:T(8,128)(2,1)} async-done(((bf16[128,4096]{0,1:T(8,128)(2,1)}), bf16[128,256]{0,1:T(8,128)(2,1)}) %reduce-scatter.4.cloned.1.call-update) | async-done | bytes 65552 | tf_op jit(solution)/shard_map/reduce_scatter | solution.py:37
  147.0 1.6 copy.21
  148.6 49.5 %reduce-scatter.6.cloned.1.call-done = bf16[128,128]{0,1:T(8,128)(2,1)} async-done(((bf16[128,1024]{0,1:T(8,128)(2,1)}), bf16[128,128]{0,1:T(8,128)(2,1)}) %reduce-scatter.6.cloned.1.call-update) | async-done | bytes 32784 | tf_op jit(solution)/shard_map/reduce_scatter | solution.py:62
  198.0 1.5 copy.22
  199.5 52.8 %reduce-scatter.8.cloned.1.call-done = bf16[8,128,128]{2,1,0:T(8,128)(2,1)} async-done(((bf16[32,128,128]{2,1,0:T(8,128)(2,1)}), bf16[8,128,128]{2,1,0:T(8,128)(2,1)}) %reduce-scatter.8.cloned.1.call-update) | async-done | bytes 262160 | tf_op jit(solution)/shard_map/reduce_scatter | solution.py:57
  252.3 1.8 fusion.6
  (5 shorter events, 0.1 us)
Async XLA Ops:
  7.2 5.3 %copy-start = (bf16[1,1,32,128,128]{4,3,2,1,0:T(8,128)(2,1)S(1)}, bf16[1,1,32,128,128]{4,3,2,1,0:T(8,128)(2,1)}, u32[]{:S(2)}) copy-start(bf16[1,1,32,128,128]{4,3,2,1,0:T(8,128)(2,1)} %param.10) | copy-start | bytes 3145732
  7.2 5.3 %copy-start.4 = (s32[1,1,2,32]{3,2,1,0:T(2,128)S(1)}, s32[1,1,2,32]{3,2,1,0:T(2,128)}, u32[]{:S(2)}) copy-start(s32[1,1,2,32]{3,2,1,0:T(2,128)} %param.11) | copy-start | bytes 772
  7.2 70.4 %all-gather.2.cloned.1.call-start = ((), (), s32[]{:S(2)}) async-start(), calls=%async_computation.4 | async-start | bytes 1114112 | tf_op jit(solution)/shard_map/all_gather | solution.py:44
  8.9 138.1 %reduce-scatter.4.cloned.1.call-start = ((), (), s32[]{:S(2)}) async-start(), calls=%async_computation.3 | async-start | bytes 1114112 | tf_op jit(solution)/shard_map/reduce_scatter | solution.py:37
  12.5 2.3 copy-start.1
  23.1 174.9 %reduce-scatter.6.cloned.1.call-start = ((), (), s32[]{:S(2)}) async-start(), calls=%async_computation.5 | async-start | bytes 294912 | tf_op jit(solution)/shard_map/reduce_scatter | solution.py:62
  80.0 1.8 copy-start.3
  81.9 5.7 %copy-start.2 = (bf16[32,128,128]{2,1,0:T(8,128)(2,1)S(1)}, bf16[32,128,128]{2,1,0:T(8,128)(2,1)}, u32[]{:S(2)}) copy-start(bf16[32,128,128]{2,1,0:T(8,128)(2,1)} %copy-done.1) | copy-start | bytes 3145732
  87.5 164.9 %reduce-scatter.8.cloned.1.call-start = ((), (), s32[]{:S(2)}) async-start(), calls=%async_computation.6 | async-start | bytes 1310720 | tf_op jit(solution)/shard_map/reduce_scatter | solution.py:57
Sparse Core Ops, SparseCore 0:
  10.7 66.8 all-gather.1
  80.4 66.5 reduce-scatter.3
  150.6 47.4 reduce-scatter.5
  200.9 51.3 reduce-scatter.7
where the time goes:
time: 261 us
  waiting for transfers between devices  213 us (82%)
  between operations  14.6 us (6%)
  other arithmetic  13.1 us (5%)
  local copies, waits for them, and re-layouts  12.6 us (5%)
  matrix products  6.87 us (3%)
    reduce_scatter x1, waiting for transfers between devices, local(): lax.psum_scatter(hidden_part.astype(jnp.bfloat16), 'col', scatter_dimensi...  56.6 us
    all_gather x1, waiting for transfers between devices, local(): lax.all_gather(grad_hidden, 'col', axis=1, tiled=True)  54.4 us
    reduce_scatter x1, waiting for transfers between devices, local(): lax.psum_scatter(slot_partial.astype(jnp.bfloat16), 'dp', scatter_dimensi...  52.8 us
    reduce_scatter x1, waiting for transfers between devices, local(): lax.psum_scatter(feature_part.astype(jnp.bfloat16), 'row', scatter_dimens...  49.5 us
    scatter-add x2, other arithmetic, masked_total(): return jax.ops.segment_sum(slot_terms, segment_ids, num_segments=segments)  9.33 us
    unnamed x14, local copies, waits for them, and re-layouts  5.84 us
  transfers between devices with their start and end apart: 4, of which 4 were waited for; matrix products, arithmetic and copies ran while one was open for 11% of the time, Pallas kernels for 0%

commit v1 on v0

--- a/solution.py
+++ b/solution.py
@@ -41,9 +41,9 @@
     owned_slots = capacity // dp_devices
     own_first = dp_index * owned_slots
     own_live = lax.dynamic_slice_in_dim(live_slots, own_first, owned_slots)
-    local_rows = lax.all_gather(grad_hidden, "col", axis=1, tiled=True).reshape(
-        token_count, row_blocks, block_size
-    )
+    local_rows = jnp.concatenate(
+        lax.all_to_all(jnp.stack([grad_hidden] * lax.axis_size("col")), "col", 0, 0), axis=1
+    ).reshape(token_count, row_blocks, block_size)
 
     def grad_terms(first_slot, number):
         picked = jnp.take(local_rows, block_rows, axis=1)

time: 261 us -> 222 us (0.85)
  waiting for transfers between devices: 213 us -> 159 us
  starting transfers between devices: 0.16 us -> 15.9 us
    all_gather x1 -> x0, waiting for transfers between devices: 54.4 us -> none  [local(): lax.all_gather(grad_hidden, 'col', axis=1, tiled=True)]
    all_to_all x0 -> x1, waiting for transfers between devices: none -> 34 us  [local(): lax.all_to_all(jnp.stack([grad_hidden] * lax.axis_size('col')), 'col', 0, 0)]
    reduce_scatter x1, waiting for transfers between devices: 56.6 us -> 23.9 us  [local(): lax.psum_scatter(hidden_part.astype(jnp.bfloat16), 'col', scatter_dimensi...]
    all_to_all x0 -> x1, starting transfers between devices: none -> 15.8 us  [local(): lax.all_to_all(jnp.stack([grad_hidden] * lax.axis_size('col')), 'col', 0, 0)]
    another operation x0 -> x2, local copies, waits for them, and re-layouts: none -> 2.82 us  [the longest x1 1.61 us: local(): local_rows = jnp.concatenate(lax.all_to_all(jnp.stack([grad_hidden] * lax...]
    unnamed x14 -> x16, local copies, waits for them, and re-layouts: 5.84 us -> 4.3 us
  transfers between devices with their start and end apart: 4 -> 4, of which waited for: 4 -> 4; matrix products, arithmetic and copies ran while one was open for 11% -> 12% of each run, Pallas kernels for 0% -> 0%
where the time goes in v1:
time: 222 us; the launch traced here: 221 us
  waiting for transfers between devices  159 us (72%)
  starting transfers between devices  15.9 us (7%)
  between operations  14.6 us (7%)
  local copies, waits for them, and re-layouts  12.3 us (6%)
  other arithmetic  12.3 us (6%)
  matrix products  6.87 us (3%)
    reduce_scatter x1, waiting for transfers between devices, local(): lax.psum_scatter(slot_partial.astype(jnp.bfloat16), 'dp', scatter_dimensi...  52.7 us
    reduce_scatter x1, waiting for transfers between devices, local(): lax.psum_scatter(feature_part.astype(jnp.bfloat16), 'row', scatter_dimens...  48.6 us
    all_to_all x1, waiting for transfers between devices, local(): lax.all_to_all(jnp.stack([grad_hidden] * lax.axis_size('col')), 'col', 0, 0)  34 us
    reduce_scatter x1, waiting for transfers between devices, local(): lax.psum_scatter(hidden_part.astype(jnp.bfloat16), 'col', scatter_dimensi...  23.9 us
    all_to_all x1, starting transfers between devices, local(): lax.all_to_all(jnp.stack([grad_hidden] * lax.axis_size('col')), 'col', 0, 0)  15.8 us
    scatter-add x2, other arithmetic, masked_total(): return jax.ops.segment_sum(slot_terms, segment_ids, num_segments=segments)  9.35 us
  transfers between devices with their start and end apart: 4, of which 4 were waited for; matrix products, arithmetic and copies ran while one was open for 12% of the time, Pallas kernels for 0%

profile of v1, /device:TPU:1, one launch (start us, length us, event | category | flops | bytes accessed | tf_op | source)
XLA Modules:
  0.0 221.3 jit_solution(10523307116246526928)
XLA Ops:
  7.2 0.0 copy-start
  7.2 0.0 copy-start.4
  7.2 1.1 copy.19
  8.2 0.0 copy-start.5
  8.3 1.2 stack.2
  9.5 15.8 %all-to-all-start = ((bf16[16,128,256]{1,2,0:T(8,128)(2,1)}), bf16[16,128,256]{1,2,0:T(8,128)(2,1)}, u32[]{:S(2)}, u32[]{:S(2)}) async-start(bf16[16,128,256]{1,2,0:T(8,128)(2,1)} %stack.2), calls=%async_computation.1 | async-start | bytes 2097152 | tf_op jit(solution)/shard_map/all_to_all | solution.py:45
  25.3 0.0 reduce-scatter.4.cloned.1.call-start
  26.0 0.0 copy-done.4
  26.0 0.2 copy.16
  26.2 0.2 copy.17
  26.3 0.0 copy-done.5
  26.4 0.7 gather_fusion
  27.1 0.0 copy-start.1
  27.2 0.0 copy-done
  27.2 2.2 %convolution_select_fusion.1 = f32[32,128,128]{2,1,0:T(8,128)} fusion(bf16[1,1,32,128,128]{4,3,2,1,0:T(8,128)(2,1)S(1)} %copy-done, pred[32]{0:T(512)(128)(4,1)S(1)} %iota_compare_fusion, bf16[32,128,128]{2,1,0:T(8,128)(2,1)S(1)} %gather_fusion, pred[32]{0:T(512)(128)(4,1)S(1)} %get-tuple-element.15), kind=kOutput, calls=%fused_computation.5 | convolution fusion | flops 135266304 | bytes 4194368 | tf_op jit(solution)/shard_map/tsm,snm->stn/dot_general | solution.py:33
  29.4 0.0 copy-done.1
  29.4 0.2 broadcast_in_dim.54
  29.6 4.7 %scatter_fusion = f32[32,128,128]{2,1,0:T(8,128)S(1)} fusion(f32[32,128,128]{2,1,0:T(8,128)S(1)} %broadcast_in_dim.54, s32[32]{0:T(128)S(1)} %get-tuple-element.18, f32[32,128,128]{2,1,0:T(8,128)} %convolution_select_fusion.1), kind=kCustom, calls=%fused_computation.2 | custom fusion | flops 524288 | bytes 6291584 | tf_op jit(solution)/shard_map/scatter-add | solution.py:12
  34.3 1.1 convert_bitcast_fusion
  35.5 2.3 %copy.18 = bf16[128,32,128]{0,2,1:T(8,128)(2,1)} copy(bf16[128,32,128]{2,0,1:T(8,128)(2,1)} %convert_bitcast_fusion) | data formatting | bytes 2097152 | tf_op jit(solution)/shard_map/convert_element_type | solution.py:38
  37.7 0.0 reduce-scatter.4.cloned.1.call-update
  37.8 0.0 reduce-scatter.6.cloned.1.call-start
  37.8 34.0 %all-to-all-done = bf16[16,128,256]{1,2,0:T(8,128)(2,1)} async-done(((bf16[16,128,256]{1,2,0:T(8,128)(2,1)}), bf16[16,128,256]{1,2,0:T(8,128)(2,1)}, u32[]{:S(2)}, u32[]{:S(2)}) %all-to-all-start) | async-done | bytes 1048608 | tf_op jit(solution)/shard_map/all_to_all | solution.py:45
  71.8 1.6 copy.20
  73.4 0.7 gather_fusion.1
  74.2 0.0 copy-start.3
  74.2 1.8 convolution_select_fusion
  76.0 0.0 copy-done.3
  76.1 0.0 copy-start.2
  76.1 4.7 %scatter_fusion.1 = f32[8,128,128]{2,1,0:T(8,128)S(1)} fusion(f32[8,128,128]{2,1,0:T(8,128)S(1)} %broadcast_in_dim.56, s32[32]{0:T(128)S(1)} %get-tuple-element.17, f32[32,128,128]{2,1,0:T(8,128)} %convolution_select_fusion), kind=kCustom, calls=%fused_computation.3 | custom fusion | flops 524288 | bytes 6291584 | tf_op jit(solution)/shard_map/scatter-add | solution.py:12
  80.8 0.9 copy.21
  81.7 0.0 reduce-scatter.6.cloned.1.call-update
  81.7 0.0 reduce-scatter.8.cloned.1.call-start
  81.7 0.0 copy-done.2
  81.8 2.8 %convolution_convert_fusion = bf16[32,128,128]{2,1,0:T(8,128)(2,1)} fusion(bf16[32,128,128]{2,1,0:T(8,128)(2,1)S(1)} %copy-done.2, pred[32]{0:T(512)(128)(4,1)S(1)} %get-tuple-element.15, bf16[32,128,128]{2,1,0:T(8,128)(2,1)} %copy-done.3, pred[32]{0:T(512)(128)(4,1)S(1)} %get-tuple-element.11), kind=kOutput, calls=%fused_computation.6 | convolution fusion | flops 135790592 | bytes 3145792 | tf_op jit(solution)/shard_map/tsn,tsm->snm/dot_general | solution.py:54
  84.6 0.0 reduce-scatter.8.cloned.1.call-update
  84.6 0.1 dynamic_slice.3
  84.7 23.9 %reduce-scatter.4.cloned.1.call-done = bf16[128,256]{0,1:T(8,128)(2,1)} async-done(((bf16[128,4096]{0,1:T(8,128)(2,1)}), bf16[128,256]{0,1:T(8,128)(2,1)}) %reduce-scatter.4.cloned.1.call-update) | async-done | bytes 65552 | tf_op jit(solution)/shard_map/reduce_scatter | solution.py:37
  108.6 1.6 copy.23
  110.2 48.6 %reduce-scatter.6.cloned.1.call-done = bf16[128,128]{0,1:T(8,128)(2,1)} async-done(((bf16[128,1024]{0,1:T(8,128)(2,1)}), bf16[128,128]{0,1:T(8,128)(2,1)}) %reduce-scatter.6.cloned.1.call-update) | async-done | bytes 32784 | tf_op jit(solution)/shard_map/reduce_scatter | solution.py:62
  158.8 1.5 copy.24
  160.3 52.7 %reduce-scatter.8.cloned.1.call-done = bf16[8,128,128]{2,1,0:T(8,128)(2,1)} async-done(((bf16[32,128,128]{2,1,0:T(8,128)(2,1)}), bf16[8,128,128]{2,1,0:T(8,128)(2,1)}) %reduce-scatter.8.cloned.1.call-update) | async-done | bytes 262160 | tf_op jit(solution)/shard_map/reduce_scatter | solution.py:57
  213.0 1.8 fusion.6
  (6 shorter events, 0.1 us)
Async XLA Ops:
  7.2 20.0 %copy-start = (bf16[1,1,32,128,128]{4,3,2,1,0:T(8,128)(2,1)S(1)}, bf16[1,1,32,128,128]{4,3,2,1,0:T(8,128)(2,1)}, u32[]{:S(2)}) copy-start(bf16[1,1,32,128,128]{4,3,2,1,0:T(8,128)(2,1)} %param.10) | copy-start | bytes 3145732
  7.2 18.8 %copy-start.4 = (bf16[128,1024]{1,0:T(8,128)(2,1)S(1)}, bf16[128,1024]{1,0:T(8,128)(2,1)}, u32[]{:S(2)}) copy-start(bf16[128,1024]{1,0:T(8,128)(2,1)} %param.9) | copy-start | bytes 786436
  8.2 18.1 %copy-start.5 = (s32[1,1,2,32]{3,2,1,0:T(2,128)S(1)}, s32[1,1,2,32]{3,2,1,0:T(2,128)}, u32[]{:S(2)}) copy-start(s32[1,1,2,32]{3,2,1,0:T(2,128)} %param.11) | copy-start | bytes 772
  9.5 62.3 %all-to-all-start = ((bf16[16,128,256]{1,2,0:T(8,128)(2,1)}), bf16[16,128,256]{1,2,0:T(8,128)(2,1)}, u32[]{:S(2)}, u32[]{:S(2)}) async-start(bf16[16,128,256]{1,2,0:T(8,128)(2,1)} %stack.2), calls=%async_computation.1 | async-start | bytes 2097152 | tf_op jit(solution)/shard_map/all_to_all | solution.py:45
  25.3 83.3 %reduce-scatter.4.cloned.1.call-start = ((), (), s32[]{:S(2)}) async-start(), calls=%async_computation.4 | async-start | bytes 1114112 | tf_op jit(solution)/shard_map/reduce_scatter | solution.py:37
  27.1 2.3 %copy-start.1 = (bf16[32,128,128]{2,1,0:T(8,128)(2,1)}, bf16[32,128,128]{2,1,0:T(8,128)(2,1)S(1)}, u32[]{:S(2)}) copy-start(bf16[32,128,128]{2,1,0:T(8,128)(2,1)S(1)} %gather_fusion) | copy-start | bytes 3145732
  37.8 121.1 %reduce-scatter.6.cloned.1.call-start = ((), (), s32[]{:S(2)}) async-start(), calls=%async_computation.5 | async-start | bytes 294912 | tf_op jit(solution)/shard_map/reduce_scatter | solution.py:62
  74.2 1.8 copy-start.3
  76.1 5.7 %copy-start.2 = (bf16[32,128,128]{2,1,0:T(8,128)(2,1)S(1)}, bf16[32,128,128]{2,1,0:T(8,128)(2,1)}, u32[]{:S(2)}) copy-start(bf16[32,128,128]{2,1,0:T(8,128)(2,1)} %copy-done.1) | copy-start | bytes 3145732
  81.7 131.3 %reduce-scatter.8.cloned.1.call-start = ((), (), s32[]{:S(2)}) async-start(), calls=%async_computation.6 | async-start | bytes 1310720 | tf_op jit(solution)/shard_map/reduce_scatter | solution.py:57
Sparse Core Ops, SparseCore 0:
  37.9 70.6 reduce-scatter.3
  112.2 46.5 reduce-scatter.5
  161.9 51.0 reduce-scatter.7
